TPU v7x, 256 devices: a whole 4x4x8 slice. The times are simulated.
256 devices in a mesh: section: 32 (over x, z_lo, core), sp: 8 (over z_hi, y).
Axes of the slice: x: 4, y: 4, z: 8 (z_hi: 2, z_lo: 4; z = z_hi * 4 + z_lo), core: 2. Of those that a mesh axis runs over, the one named last changes fastest.
Arguments:
- segment_starting_activations: bfloat16 [32, 256, 2560], P('section', 'sp'), may hold values from -40 to 40
- prior_step_memory_pairs: bfloat16 [32, 2, 768, 3072], P('section', None, None, 'sp'), may hold values from -3 to 3
- triple_projection_matrix: bfloat16 [32, 2560, 3, 3072], P('section', None, None, 'sp'), may hold values from -0.125 to 0.125
- final_projection_matrix: bfloat16 [32, 3072, 2560], P('section', 'sp'), may hold values from -0.109375 to 0.109375
- layer_gain_factors: float32 [32, 2560], P('section'), may hold values from 0.5 to 2
- tile_element_counts: int32 [4], replicated, may hold values from 1 to 256, 768 in all
- tile_visit_order: int32 [4], replicated, may hold values from 0 to 3, each once
Outputs:
- outflight: bfloat16 [32, 256, 2560], P('section', 'sp')
- new_cache: bfloat16 [32, 2, 768, 3072], P('section', None, None, 'sp')
Inputs may be any that keep to these rules, and one draw needn't show every extreme that they name: `tile_element_counts`: the patches cover the 768 tokens of the clip in order; the entries sum to 768 and the largest is 256. `tile_visit_order`: each patch appears once.
All inputs are finite; a program needn't handle non-finite values.
Results may differ from a plain program's by a relative error of at most 0.022.
Values may be sent and summed in bfloat16 or wider, within the bound.
A program may use at most 64 MiB of HBM per device.

v0:
```python
import math

import jax
import jax.numpy as jnp
from jax import lax
from jax.sharding import PartitionSpec as P

HD = 128
TICKS = 4


SCORE_GAIN = 2.5
EPSILON = 1e-06


def passed_along(value, axis, steps):
    count = lax.axis_size(axis)
    pairs = [(source, (source + steps) % count) for source in range(count)]
    return lax.ppermute(value, axis, pairs)


def rms_rows(values, gain_row):
    widened = values.astype(jnp.float32)
    spread = jnp.mean(widened * widened, axis=-1, keepdims=True)
    return (widened * lax.rsqrt(spread + EPSILON) * gain_row).astype(jnp.bfloat16)


def plan(lengths, order, section_id, tick_step):
    slot_ids = jnp.arange(lengths.shape[0], dtype=jnp.int32)
    slot_id = (section_id - tick_step) % lengths.shape[0]
    patch_id = jnp.sum(jnp.where(slot_ids == slot_id, order, 0))
    length = jnp.sum(jnp.where(slot_ids == patch_id, lengths, 0))
    first_row = jnp.sum(jnp.where(slot_ids < patch_id, lengths, 0))
    return (first_row, length)


def head_norm(values, head_count):
    shaped = values.reshape(values.shape[0], head_count, HD)
    spread = jnp.mean(shaped * shaped, axis=-1, keepdims=True)
    return (shaped * lax.rsqrt(spread + EPSILON)).astype(jnp.bfloat16)


def refresh(kv_store, fresh, first_row, length):
    summed = kv_store.shape[1]
    padded = jnp.concatenate([kv_store, jnp.zeros_like(fresh)], axis=1)
    window = lax.dynamic_slice_in_dim(padded, first_row, fresh.shape[1], 1)
    keep_rows = jnp.arange(fresh.shape[1], dtype=jnp.int32) < length
    window = jnp.where(keep_rows[None, :, None], fresh, window)
    padded = lax.dynamic_update_slice_in_dim(padded, window, first_row, 1)
    return padded[:, :summed]


def layer_core(projected, kv_store, first_row, length):
    inner_width = kv_store.shape[2]
    head_count = inner_width // HD
    queries = head_norm(projected[:, :inner_width], head_count)
    key_new = head_norm(projected[:, inner_width : 2 * inner_width], head_count).reshape(
        -1, inner_width
    )
    value_new = projected[:, 2 * inner_width :].astype(jnp.bfloat16)
    kv_store = refresh(kv_store, jnp.stack([key_new, value_new]), first_row, length)
    key_all = kv_store[0].reshape(-1, head_count, HD)
    value_all = kv_store[1].reshape(-1, head_count, HD)
    scores = jnp.einsum("qhd,khd->hqk", queries, key_all, preferred_element_type=jnp.float32) * (
        SCORE_GAIN / math.sqrt(HD)
    )
    weights = jnp.exp(scores)
    probabilities = (weights / jnp.sum(weights, axis=-1, keepdims=True)).astype(jnp.bfloat16)
    attended = jnp.einsum(
        "hqk,khd->qhd", probabilities, value_all, preferred_element_type=jnp.float32
    )
    return (attended.astype(jnp.bfloat16).reshape(-1, inner_width), kv_store)


def local(
    segment_starting_activations,
    prior_step_memory_pairs,
    triple_projection_matrix,
    final_projection_matrix,
    layer_gain_factors,
    tile_element_counts,
    tile_visit_order,
):
    model_dimension = segment_starting_activations.shape[2]
    segment_entries = segment_starting_activations.shape[1]
    inner_width = final_projection_matrix.shape[1]
    w_project = triple_projection_matrix.reshape(model_dimension, 3 * inner_width)
    w_output = final_projection_matrix.reshape(inner_width, model_dimension)
    kv_store = prior_step_memory_pairs[0]
    section_id = lax.axis_index("section")
    current_entries = lax.all_gather(segment_starting_activations[0], "sp", axis=0, tiled=True)
    for tick_step in range(TICKS):
        first_row, length = plan(tile_element_counts, tile_visit_order, section_id, tick_step)
        normed = rms_rows(current_entries, layer_gain_factors)
        projected = jnp.dot(normed, w_project, preferred_element_type=jnp.float32)
        attended, kv_store = layer_core(projected, kv_store, first_row, length)
        partial_value = jnp.dot(attended, w_output, preferred_element_type=jnp.float32)
        summed = lax.psum(partial_value.astype(jnp.bfloat16), "sp").astype(jnp.float32)
        updated = (current_entries.astype(jnp.float32) + summed).astype(jnp.bfloat16)
        current_entries = passed_along(updated, "section", 1)
    sp_index = lax.axis_index("sp")
    result = lax.dynamic_slice_in_dim(
        current_entries, sp_index * segment_entries, segment_entries, 0
    )
    return (result[None], kv_store[None])


def solution(mesh):
    placed = (
        P("section", "sp", None),
        P("section", None, None, "sp"),
        P("section", None, None, "sp"),
        P("section", "sp", None),
        P("section", None),
        P(),
        P(),
    )
    return jax.shard_map(
        local,
        mesh=mesh,
        in_specs=placed,
        out_specs=(P("section", "sp", None), P("section", None, None, "sp")),
        check_vma=False,
    )
```

profile of v0, /device:TPU:227, one launch (start us, length us, event | category | flops | bytes accessed | tf_op | source)
XLA Modules:
  0.0 768.8 jit_solution(13511223934003232585)
XLA Ops:
  9.4 3.9 fusion.75
  14.7 8.9 %copy.25 = bf16[1,2560,3,384]{1,3,2,0:T(8,128)(2,1)} copy(bf16[1,2560,3,384]{3,1,2,0:T(8,128)(2,1)} %param.9) | data formatting | bytes 11796480 | tf_op args[2]
  26.9 43.4 %all-gather.3.cloned.1.call-done = bf16[1,256,2560]{2,1,0:T(8,128)(2,1)} async-done(((bf16[1,32,2560]{2,1,0:T(8,128)(2,1)}), bf16[1,256,2560]{2,1,0:T(8,128)(2,1)}) %all-gather.3.cloned.1.call-update) | async-done | bytes 1310736 | tf_op jit(solution)/shard_map/all_gather | solution.py:91
  72.0 5.0 fusion.24
  84.5 2.2 fusion.88
  89.7 2.2 maximum_select_fusion
  91.8 3.2 dynamic_update_slice.12
  96.4 2.2 copy.30
  105.4 114.5 %all-reduce.6.cloned.1.call-done = bf16[256,2560]{1,0:T(8,128)(2,1)} async-done(((bf16[256,2560]{1,0:T(8,128)(2,1)}), bf16[256,2560]{1,0:T(8,128)(2,1)}) %all-reduce.6.cloned.1.call-update) | async-done | bytes 1310736 | tf_op jit(solution)/shard_map/psum | solution.py:98
  219.9 2.7 fusion.15
  222.7 6.8 collective-permute-start
  234.2 10.1 %collective-permute-done = bf16[256,2560]{1,0:T(8,128)(2,1)} collective-permute-done((bf16[256,2560]{1,0:T(8,128)(2,1)}, bf16[256,2560]{1,0:T(8,128)(2,1)}, u32[]{:S(2)}, u32[]{:S(2)}) %collective-permute-start) | collective-permute-done | bytes 1310752 | tf_op jit(solution)/shard_map/ppermute | solution.py:19
  246.0 5.0 fusion.30
  258.5 2.1 fusion.87
  265.6 3.2 dynamic_update_slice.13
  278.9 115.1 %all-reduce.8.cloned.1.call-done = bf16[256,2560]{1,0:T(8,128)(2,1)} async-done(((bf16[256,2560]{1,0:T(8,128)(2,1)}), bf16[256,2560]{1,0:T(8,128)(2,1)}) %all-reduce.8.cloned.1.call-update) | async-done | bytes 1310736 | tf_op jit(solution)/shard_map/psum | solution.py:98
  394.0 3.1 fusion.3
  397.1 6.8 collective-permute-start.1
  408.6 10.2 %collective-permute-done.1 = bf16[256,2560]{1,0:T(8,128)(2,1)} collective-permute-done((bf16[256,2560]{1,0:T(8,128)(2,1)}, bf16[256,2560]{1,0:T(8,128)(2,1)}, u32[]{:S(2)}, u32[]{:S(2)}) %collective-permute-start.1) | collective-permute-done | bytes 1310752 | tf_op jit(solution)/shard_map/ppermute | solution.py:19
  420.5 5.0 fusion.28
  429.7 2.1 fusion.86
  436.8 3.2 dynamic_update_slice.14
  450.1 115.1 %all-reduce.10.cloned.1.call-done = bf16[256,2560]{1,0:T(8,128)(2,1)} async-done(((bf16[256,2560]{1,0:T(8,128)(2,1)}), bf16[256,2560]{1,0:T(8,128)(2,1)}) %all-reduce.10.cloned.1.call-update) | async-done | bytes 1310736 | tf_op jit(solution)/shard_map/psum | solution.py:98
  565.1 3.1 fusion.7
  568.3 6.8 collective-permute-start.2
  579.5 10.4 %collective-permute-done.2 = bf16[256,2560]{1,0:T(8,128)(2,1)} collective-permute-done((bf16[256,2560]{1,0:T(8,128)(2,1)}, bf16[256,2560]{1,0:T(8,128)(2,1)}, u32[]{:S(2)}, u32[]{:S(2)}) %collective-permute-start.2) | collective-permute-done | bytes 1310752 | tf_op jit(solution)/shard_map/ppermute | solution.py:19
  591.6 5.0 fusion.26
  607.8 3.2 dynamic_update_slice.15
  621.0 115.0 %all-reduce.12.cloned.1.call-done = bf16[256,2560]{1,0:T(8,128)(2,1)} async-done(((bf16[256,2560]{1,0:T(8,128)(2,1)}), bf16[256,2560]{1,0:T(8,128)(2,1)}) %all-reduce.12.cloned.1.call-update) | async-done | bytes 1310736 | tf_op jit(solution)/shard_map/psum | solution.py:98
  736.0 3.1 fusion.11
  739.1 6.8 collective-permute-start.3
  747.0 13.7 %collective-permute-done.3 = bf16[256,2560]{1,0:T(8,128)(2,1)} collective-permute-done((bf16[256,2560]{1,0:T(8,128)(2,1)}, bf16[256,2560]{1,0:T(8,128)(2,1)}, u32[]{:S(2)}, u32[]{:S(2)}) %collective-permute-start.3) | collective-permute-done | bytes 1310752 | tf_op jit(solution)/shard_map/ppermute | solution.py:19
  (133 shorter events, 103.7 us)
Async XLA Ops:
  7.2 96.2 %copy-start = (bf16[1,384,2560]{2,1,0:T(8,128)(2,1)S(1)}, bf16[1,384,2560]{2,1,0:T(8,128)(2,1)}, u32[]{:S(2)}) copy-start(bf16[1,384,2560]{2,1,0:T(8,128)(2,1)} %param.10) | copy-start | bytes 5898244
  7.2 63.1 %all-gather.3.cloned.1.call-start = ((), (), s32[]{:S(2)}) async-start(), calls=%async_computation.4 | async-start | bytes 1474560 | tf_op jit(solution)/shard_map/all_gather | solution.py:91
  7.9 212.0 %all-reduce.6.cloned.1.call-start = ((), (), s32[]{:S(2)}) async-start(), calls=%async_computation | async-start | bytes 2621440 | tf_op jit(solution)/shard_map/psum | solution.py:98
  14.7 9.6 %copy-start.13 = (f32[1,2560]{1,0:T(1,128)S(1)}, f32[1,2560]{1,0:T(1,128)}, u32[]{:S(2)}) copy-start(f32[1,2560]{1,0:T(1,128)} %param.11) | copy-start | bytes 30724
  77.0 1.1 copy-start.6
  95.1 5.6 copy-start.3
  100.7 1.9 copy-start.9
  103.3 116.6 %copy-start.4 = (bf16[1,256,2560]{2,1,0:T(8,128)(2,1)S(1)}, bf16[1,256,2560]{2,1,0:T(8,128)(2,1)}, u32[]{:S(2)}) copy-start(bf16[1,256,2560]{2,1,0:T(8,128)(2,1)} %all-gather.3.cloned.1.call-done) | copy-start | bytes 3932164
  105.4 127.2 %copy-start.14 = (pred[1024]{0:T(1024)(128)(4,1)S(1)}, pred[1024]{0:T(1024)(128)(4,1)}, u32[]{:S(2)}) copy-start(pred[1024]{0:T(1024)(128)(4,1)} %constant.72.clone.1) | copy-start | bytes 3076
  105.4 288.6 %all-reduce.8.cloned.1.call-start = ((), (), s32[]{:S(2)}) async-start(), calls=%async_computation.1 | async-start | bytes 2621440 | tf_op jit(solution)/shard_map/psum | solution.py:98
  222.7 21.6 %collective-permute-start = (bf16[256,2560]{1,0:T(8,128)(2,1)}, bf16[256,2560]{1,0:T(8,128)(2,1)}, u32[]{:S(2)}, u32[]{:S(2)}) collective-permute-start(bf16[256,2560]{1,0:T(8,128)(2,1)} %fusion.15), channel_id=1, source_target_pairs={{0,8},{8,16},{16,24},{24,32},{32,40},{40,48},{48,56},{56,64},{64,7... | collective-permute-start | bytes 3932168 | tf_op jit(solution)/shard_map/ppermute | solution.py:19
  251.0 1.1 copy-start.7
  274.2 1.9 copy-start.10
  278.8 128.3 %copy-start.15 = (pred[1024]{0:T(1024)(128)(4,1)S(1)}, pred[1024]{0:T(1024)(128)(4,1)}, u32[]{:S(2)}) copy-start(pred[1024]{0:T(1024)(128)(4,1)} %constant.72.clone.1) | copy-start | bytes 3076
  278.8 286.3 %all-reduce.10.cloned.1.call-start = ((), (), s32[]{:S(2)}) async-start(), calls=%async_computation.2 | async-start | bytes 2621440 | tf_op jit(solution)/shard_map/psum | solution.py:98
  397.1 21.6 %collective-permute-start.1 = (bf16[256,2560]{1,0:T(8,128)(2,1)}, bf16[256,2560]{1,0:T(8,128)(2,1)}, u32[]{:S(2)}, u32[]{:S(2)}) collective-permute-start(bf16[256,2560]{1,0:T(8,128)(2,1)} %fusion.3), channel_id=1, source_target_pairs={{0,8},{8,16},{16,24},{24,32},{32,40},{40,48},{48,56},{56,64},{64,7... | collective-permute-start | bytes 3932168 | tf_op jit(solution)/shard_map/ppermute | solution.py:19
  425.5 1.1 copy-start.8
  427.6 7.2 copy-start.1
  445.4 1.9 copy-start.11
  450.0 128.1 %copy-start.16 = (pred[1024]{0:T(1024)(128)(4,1)S(1)}, pred[1024]{0:T(1024)(128)(4,1)}, u32[]{:S(2)}) copy-start(pred[1024]{0:T(1024)(128)(4,1)} %constant.72.clone.1) | copy-start | bytes 3076
  450.0 285.9 %all-reduce.12.cloned.1.call-start = ((), (), s32[]{:S(2)}) async-start(), calls=%async_computation.3 | async-start | bytes 2621440 | tf_op jit(solution)/shard_map/psum | solution.py:98
  568.3 21.6 %collective-permute-start.2 = (bf16[256,2560]{1,0:T(8,128)(2,1)}, bf16[256,2560]{1,0:T(8,128)(2,1)}, u32[]{:S(2)}, u32[]{:S(2)}) collective-permute-start(bf16[256,2560]{1,0:T(8,128)(2,1)} %fusion.7), channel_id=1, source_target_pairs={{0,8},{8,16},{16,24},{24,32},{32,40},{40,48},{48,56},{56,64},{64,7... | collective-permute-start | bytes 3932168 | tf_op jit(solution)/shard_map/ppermute | solution.py:19
  596.6 1.1 copy-start.5
  598.7 7.1 copy-start.2
  598.7 7.2 copy-start.17
  616.4 1.9 copy-start.12
  739.1 21.6 %collective-permute-start.3 = (bf16[256,2560]{1,0:T(8,128)(2,1)}, bf16[256,2560]{1,0:T(8,128)(2,1)}, u32[]{:S(2)}, u32[]{:S(2)}) collective-permute-start(bf16[256,2560]{1,0:T(8,128)(2,1)} %fusion.11), channel_id=1, source_target_pairs={{0,8},{8,16},{16,24},{24,32},{32,40},{40,48},{48,56},{56,64},{64,7... | collective-permute-start | bytes 3932168 | tf_op jit(solution)/shard_map/ppermute | solution.py:19
Sparse Core Ops, SparseCore 0:
  10.6 59.6 all-gather.2
  105.5 114.3 all-reduce.5
  278.9 115.0 all-reduce.7
  450.1 114.9 all-reduce.9
  621.1 114.7 all-reduce.11
where the time goes:
time: 779 us; the launch traced here: 769 us
  waiting for transfers between devices  548 us (70%)
  local copies, waits for them, and re-layouts  75 us (10%)
  other arithmetic  57.9 us (7%)
  matrix products  38.4 us (5%)
  starting transfers between devices  27.3 us (4%)
  between operations  22 us (3%)
    psum x4, waiting for transfers between devices, local(): lax.psum(partial_value.astype(jnp.bfloat16), 'sp').astype(jnp.float32)  460 us
    ppermute x4, waiting for transfers between devices, passed_along(): return lax.ppermute(value, axis, pairs)  44.4 us
    all_gather x1, waiting for transfers between devices, local(): lax.all_gather(segment_starting_activations[0], 'sp', axis=0, tiled=True)  43.4 us
    ppermute x4, starting transfers between devices, passed_along(): return lax.ppermute(value, axis, pairs)  27.1 us
    dot_general x4, matrix products, local(): projected = jnp.dot(normed, w_project, preferred_element_type=jnp.float32)  20 us
  transfers between devices with their start and end apart: 9, of which 9 were waited for; matrix products, arithmetic and copies ran while one was open for 3% of the time, Pallas kernels for 0%

commit v1 on v0

v1 whole, which is shorter than its diff:
```python
import functools
import math

import jax
import jax.numpy as jnp
from jax import lax
from jax.experimental import pallas as pl
from jax.experimental.pallas import tpu as pltpu
from jax.sharding import PartitionSpec as P

HD = 128
TICKS = 4
SCORE_GAIN = 2.5
EPSILON = 1e-06
PIECE = 16
SHIFT = 16.0
MESH = pl.DeviceIdType.MESH


def relay_kernel(
    n_sections, counts_ref, order_ref, x0_ref, kv_hbm, wqkv_hbm, wout_hbm, gain_ref, out_ref, kv_out,
    X, PA, R3, RL, EX, S, W, WO, KV, Q, KF, VF, O, L, wsem, xsem, ss, zs, zs0, r3s, rls, exs, ags, osem,
):
    model = X.shape[-1]
    inner = KV.shape[-1]
    heads = inner // HD
    tokens = KV.shape[1]
    NP = PA.shape[1]
    NB = NP // 2
    rows = 4 * PIECE
    patches = order_ref.shape[0]

    section, sp = lax.axis_index("section"), lax.axis_index("sp")
    zh, y = sp // 4, sp % 4
    later, before = (section + 1) % n_sections, (section + n_sections - 1) % n_sections
    up, down = (section, zh * 4 + (y + 1) % 4), (section, zh * 4 + (y + 3) % 4)
    across = (section, (1 - zh) * 4 + y)
    next_same, next_other = (later, zh * 4 + y), (later, (1 - zh) * 4 + y)

    def send(src, dst, send_sem, recv_sem, device):
        pltpu.make_async_remote_copy(
            src_ref=src, dst_ref=dst, send_sem=send_sem, recv_sem=recv_sem, device_id=device, device_id_type=MESH
        ).start()

    def take(view, sem):
        pltpu.make_async_copy(view, view, sem).wait()

    def take_pieces(count, sem):
        take(X.at[pl.ds(0, count // 4)] if count % 4 == 0 else X.at[0, pl.ds(0, count)], sem)

    loads = [pltpu.make_async_copy(kv_hbm.at[0], KV, wsem.at[4])]
    for j in range(3):
        loads.append(pltpu.make_async_copy(wqkv_hbm.at[0, j], W.at[:, pl.ds(j * inner, inner)], wsem.at[j]))
    loads.append(pltpu.make_async_copy(wout_hbm.at[0], WO, wsem.at[3]))
    starts = [
        pltpu.make_async_copy(x0_ref.at[0, pl.ds(k * PIECE, PIECE)], X.at[zh * NB + k, 0], xsem.at[k]) for k in range(NB)
    ]
    for copy in starts + loads:
        copy.start()

    barrier = pltpu.get_barrier_semaphore()
    friends = [up, down, across, next_same, next_other, (before, zh * 4 + y), (before, (1 - zh) * 4 + y)]
    for device in friends:
        pl.semaphore_signal(barrier, inc=1, device_id=device, device_id_type=MESH)
    pl.semaphore_wait(barrier, len(friends))

    for copy in starts:
        copy.wait()
    for k in range(NB):
        piece = X.at[zh * NB + k, 0]
        send(piece, piece, zs0, exs.at[0, zh * NB + k], across)
    for copy in loads:
        copy.wait()

    local = lax.broadcasted_iota(jnp.int32, (1, NP * rows), 1)
    slot = (local % rows) // PIECE
    chunk = (y + jnp.where(slot == 1, 1, jnp.where(slot == 2, 3, jnp.where(slot == 3, 2, 0)))) % 4
    within = (local // rows) * PIECE + local % PIECE
    global_row = (within // 32) * 128 + chunk * 32 + within % 32
    token = lax.broadcasted_iota(jnp.int32, (1, tokens), 1)
    gain = gain_ref[...]
    factor = SCORE_GAIN / math.sqrt(HD) * math.log2(math.e)
    shift = SHIFT * math.log2(math.e)

    def head_norm(part):
        spread = jnp.mean(part * part, axis=-1, keepdims=True)
        return (part * lax.rsqrt(spread + EPSILON)).astype(jnp.bfloat16)

    def scores(query, keys, bias):
        s = lax.dot_general(query, keys, (((1,), (1,)), ((), ())), preferred_element_type=jnp.float32)
        return jnp.exp2(s * factor + bias)

    def tick(t, _):
        patch = order_ref[(section + TICKS * n_sections - t) % patches]
        length, first = jnp.int32(0), jnp.int32(0)
        for r in range(patches):
            length = length + jnp.where(patch == r, counts_ref[r], 0)
            first = first + jnp.where(r < patch, counts_ref[r], 0)
        held_bias = jnp.where((token >= first) & (token < first + length), -1e30, -shift)
        fresh_bias = jnp.where(global_row < length, -shift, -1e30)

        def place(i):
            return (i + jnp.where(t == 0, zh * NB, 0)) % NP

        def stage_f(i):
            ii = place(i)
            if i >= NB:
                @pl.when(t == 0)
                def _():
                    take(X.at[ii, 0], exs.at[0, ii])

            @pl.when(t > 0)
            def _():
                take(EX.at[t, i], exs.at[t, i])
                total = EX[t, i, 0].astype(jnp.float32) + EX[t, i, 1].astype(jnp.float32)
                X[t * NP + ii, 0] = total.astype(jnp.bfloat16)

            at = t * NP + ii
            send(X.at[at, 0], X.at[at, 2], ss.at[t], ags.at[t, ii, 2], up)
            send(X.at[at, 0], X.at[at, 1], ss.at[t], ags.at[t, ii, 1], down)

        def stage_g(i):
            ii = place(i)
            at = t * NP + ii
            source, device = (2, up) if i % 2 == 0 else (1, down)
            take(X.at[at, source], ags.at[t, ii, source])
            send(X.at[at, source], X.at[at, 3], ss.at[t], ags.at[t, ii, 3], device)

        def stage_h(i):
            ii = place(i)
            at = t * NP + ii
            other = 1 if i % 2 == 0 else 2
            take(X.at[at, other], ags.at[t, ii, other])
            take(X.at[at, 3], ags.at[t, ii, 3])
            x = X[at].reshape(rows, model).astype(jnp.float32)
            spread = jnp.mean(x * x, axis=-1, keepdims=True)
            normed = (x * lax.rsqrt(spread + EPSILON) * gain).astype(jnp.bfloat16)
            here = pl.ds(pl.multiple_of(ii * rows, rows), rows)
            parts = [
                jnp.dot(normed, W[:, j * inner : (j + 1) * inner], preferred_element_type=jnp.float32) for j in range(3)
            ]
            VF[here, :] = parts[2].astype(jnp.bfloat16)
            for h in range(heads):
                cols = slice(h * HD, (h + 1) * HD)
                query = head_norm(parts[0][:, cols])
                Q[here, cols] = query
                KF[here, cols] = head_norm(parts[1][:, cols])
                e = scores(query, KV[0, :, cols], held_bias)
                L[here, cols] = jnp.broadcast_to(jnp.sum(e, axis=-1, keepdims=True), (rows, HD))
                O[here, cols] = jnp.dot(e.astype(jnp.bfloat16), KV[1, :, cols], preferred_element_type=jnp.float32)

        def stage_c(i):
            here = slice(i * rows, (i + 1) * rows)
            attended = []
            for h in range(heads):
                cols = slice(h * HD, (h + 1) * HD)
                e = scores(Q[here, cols], KF[:, cols], fresh_bias)
                total = L[here, cols] + jnp.sum(e, axis=-1, keepdims=True)
                mixed = O[here, cols] + jnp.dot(
                    e.astype(jnp.bfloat16), VF[:, cols], preferred_element_type=jnp.float32
                )
                attended.append((mixed / total).astype(jnp.bfloat16))
            partial = jnp.dot(jnp.concatenate(attended, axis=1), WO[...], preferred_element_type=jnp.float32)
            PA[t, i] = partial.astype(jnp.bfloat16).reshape(4, PIECE, model)
            if i % 2 == 0:
                send(PA.at[t, i, 3], R3.at[t, i], ss.at[t], r3s.at[t, i], up)
                send(PA.at[t, i, 2], RL.at[t, i, 1], ss.at[t], rls.at[t, i], down)
            else:
                send(PA.at[t, i, 3], R3.at[t, i], ss.at[t], r3s.at[t, i], down)
                send(PA.at[t, i, 1], RL.at[t, i, 0], ss.at[t], rls.at[t, i], up)

        def stage_d(i):
            take(R3.at[t, i], r3s.at[t, i])
            mine, side, device = (1, 0, up) if i % 2 == 0 else (2, 1, down)
            total = PA[t, i, mine].astype(jnp.float32) + R3[t, i].astype(jnp.float32)
            PA[t, i, mine] = total.astype(jnp.bfloat16)
            send(PA.at[t, i, mine], RL.at[t, i, side], ss.at[t], rls.at[t, i], device)

        def stage_e(i):
            take(RL.at[t, i], rls.at[t, i])
            total = PA[t, i, 0].astype(jnp.float32) + RL[t, i, 0].astype(jnp.float32) + RL[t, i, 1].astype(jnp.float32)
            total = total + jnp.where(zh == i // NB, X[t * NP + i, 0].astype(jnp.float32), 0.0)
            S[t, i] = total.astype(jnp.bfloat16)

            @pl.when(t < TICKS - 1)
            def _():
                send(S.at[t, i], EX.at[t + 1, i, 0], zs.at[t], exs.at[t + 1, i], next_same)
                send(S.at[t, i], EX.at[t + 1, i, 1], zs.at[t], exs.at[t + 1, i], next_other)

            @pl.when(t == TICKS - 1)
            def _():
                k = i % NB
                send(S.at[t, i], EX.at[TICKS, k, zh], zs.at[t], exs.at[TICKS, k], (later, (i // NB) * 4 + y))

        def update():
            for b in range(3):
                span = tokens // 3
                at = pl.ds(b * span, span)
                row = lax.broadcasted_iota(jnp.int32, (span, 1), 0) + (b * span - first)
                hit = (row == global_row) & (global_row < length)
                pick = jnp.where(hit, 1.0, 0.0).astype(jnp.bfloat16)
                inside = (row >= 0) & (row < length)
                for part, fresh in ((0, KF), (1, VF)):
                    moved = jnp.dot(pick, fresh[...], preferred_element_type=jnp.float32)
                    kept = KV[part, at, :].astype(jnp.float32)
                    KV[part, at, :] = jnp.where(inside, moved, kept).astype(jnp.bfloat16)

        stage_f(0)
        for i in range(1, NP):
            stage_f(i)
            stage_g(i - 1)
            if i >= 2:
                stage_h(i - 2)
        stage_g(NP - 1)
        stage_h(NP - 2)
        stage_h(NP - 1)
        for i in range(NP):
            stage_c(i)
        stage_d(0)
        for i in range(1, NP):
            stage_d(i)
            stage_e(i - 1)
        stage_e(NP - 1)
        update()
        return 0

    lax.fori_loop(0, TICKS, tick, 0)
    cache_out = pltpu.make_async_copy(KV, kv_out.at[0], osem)
    cache_out.start()
    for k in range(NB):
        take(EX.at[TICKS, k], exs.at[TICKS, k])
        total = EX[TICKS, k, 0].astype(jnp.float32) + EX[TICKS, k, 1].astype(jnp.float32)
        out_ref[0, pl.ds(k * PIECE, PIECE), :] = total.astype(jnp.bfloat16)
    take_pieces(NB, zs0)
    for t in range(TICKS):
        take_pieces(6 * NP, ss.at[t])
        take_pieces(2 * NP if t < TICKS - 1 else NP, zs.at[t])
    cache_out.wait()


def local(n_sections, x0, kv, wqkv, wout, gain, counts, order):
    entries, model = x0.shape[1:]
    tokens, inner = kv.shape[2:]
    NP = 2 * entries // PIECE
    NB = NP // 2
    rows = 8 * entries
    bf16, f32 = jnp.bfloat16, jnp.float32
    piece = (PIECE, model)
    dma = pltpu.SemaphoreType.DMA
    any_space = pl.BlockSpec(memory_space=pl.ANY)
    vmem = pl.BlockSpec(memory_space=pltpu.VMEM)
    smem = pl.BlockSpec(memory_space=pltpu.SMEM)
    return pl.pallas_call(
        functools.partial(relay_kernel, n_sections),
        out_shape=(
            jax.ShapeDtypeStruct((1, entries, model), bf16),
            jax.ShapeDtypeStruct((1, 2, tokens, inner), bf16),
        ),
        in_specs=[smem, smem, any_space, any_space, any_space, any_space, vmem],
        out_specs=(vmem, any_space),
        scratch_shapes=[
            pltpu.VMEM((TICKS * NP, 4) + piece, bf16),
            pltpu.VMEM((TICKS, NP, 4) + piece, bf16),
            pltpu.VMEM((TICKS, NP) + piece, bf16),
            pltpu.VMEM((TICKS, NP, 2) + piece, bf16),
            pltpu.VMEM((TICKS + 1, NP, 2) + piece, bf16),
            pltpu.VMEM((TICKS, NP) + piece, bf16),
            pltpu.VMEM((model, 3 * inner), bf16),
            pltpu.VMEM((inner, model), bf16),
            pltpu.VMEM((2, tokens, inner), bf16),
            pltpu.VMEM((rows, inner), bf16),
            pltpu.VMEM((rows, inner), bf16),
            pltpu.VMEM((rows, inner), bf16),
            pltpu.VMEM((rows, inner), f32),
            pltpu.VMEM((rows, inner), f32),
            dma((5,)), dma((NB,)), dma((TICKS,)), dma((TICKS,)), dma,
            dma((TICKS, NP)), dma((TICKS, NP)), dma((TICKS + 1, NP)), dma((TICKS, NP, 4)), dma,
        ],
        compiler_params=pltpu.CompilerParams(
            collective_id=0, has_side_effects=True, vmem_limit_bytes=56 * 1024 * 1024
        ),
    )(counts, order, x0, kv, jnp.transpose(wqkv, (0, 2, 1, 3)), wout, gain)


def solution(mesh):
    placed = (
        P("section", "sp", None),
        P("section", None, None, "sp"),
        P("section", None, None, "sp"),
        P("section", "sp", None),
        P("section", None),
        P(),
        P(),
    )
    return jax.shard_map(
        functools.partial(local, mesh.shape["section"]),
        mesh=mesh,
        in_specs=placed,
        out_specs=(P("section", "sp", None), P("section", None, None, "sp")),
        check_vma=False,
    )
```

time: 779 us -> 171 us (0.22)
  waiting for transfers between devices: 548 us -> 0 us
  Pallas kernels: 0 us -> 163 us
  local copies, waits for them, and re-layouts: 75 us -> 3.99 us
  other arithmetic: 57.9 us -> 0 us
  matrix products: 38.4 us -> 0 us
  starting transfers between devices: 27.3 us -> 0 us
  between operations: 22 us -> 0.64 us
    psum x4 -> x0, waiting for transfers between devices: 460 us -> none  [local(): lax.psum(partial_value.astype(jnp.bfloat16), 'sp').astype(jnp.float32)]
    pallas_call x0 -> x1, Pallas kernels: none -> 163 us  [local(): pl.pallas_call(functools.partial(relay_kernel, n_sections), out_shape=(ja...]
    ppermute x4 -> x0, waiting for transfers between devices: 44.4 us -> none  [passed_along(): return lax.ppermute(value, axis, pairs)]
    all_gather x1 -> x0, waiting for transfers between devices: 43.4 us -> none  [local(): lax.all_gather(segment_starting_activations[0], 'sp', axis=0, tiled=True)]
    dot_general x16 -> x0, matrix products: 38.4 us -> none  [the longest x4 20 us: local(): projected = jnp.dot(normed, w_project, preferred_element_type=jnp.float32)]
    slice x16 -> x0, local copies, waits for them, and re-layouts: 29.4 us -> none  [the longest x8 13.3 us: layer_core(): key_all = kv_store[0].reshape(-1, head_count, HD)]
    ppermute x4 -> x0, starting transfers between devices: 27.1 us -> none  [passed_along(): return lax.ppermute(value, axis, pairs)]
    reduce_sum x14 -> x0, other arithmetic: 18.2 us -> none  [the longest x4 6.61 us: rms_rows(): spread = jnp.mean(widened * widened, axis=-1, keepdims=True)]
  transfers between devices with their start and end apart: 9 -> 0, of which waited for: 9 -> 0; matrix products, arithmetic and copies ran while one was open for 3% -> 0% of each run, Pallas kernels for 0% -> 0%
where the time goes in v1:
time: 171 us; the launch traced here: 168 us
  Pallas kernels  163 us (95%)
  local copies, waits for them, and re-layouts  3.99 us (2%)
    pallas_call x1, Pallas kernels, local(): pl.pallas_call(functools.partial(relay_kernel, n_sections), out_shape=(ja...  163 us
    unnamed x2, local copies, waits for them, and re-layouts  3.99 us

profile of v1, /device:TPU:227, one launch (start us, length us, event | category | flops | bytes accessed | tf_op | source)
XLA Modules:
  0.0 167.8 jit_solution(16129165921852330831)
XLA Ops:
  0.6 163.1 %shard_map.86 = (bf16[1,32,2560]{2,1,0:T(8,128)(2,1)}, bf16[1,2,768,384]{3,2,1,0:T(8,128)(2,1)}) custom-call(s32[4]{0:T(128)} %counts_ref.1, s32[4]{0:T(128)} %order_ref.1, bf16[1,32,2560]{2,1,0:T(8,128)(2,1)} %x0_ref.1, bf16[1,2,768,384]{3,2,1,0:T(8,128)(2,1)} %kv_hbm.1, bf16[1,3,2560,384]{3,2,1,0:T(8,128)(2,1)} %bitcast.1, bf16[1,384,2560]{2,1,0:T(8,128)(2,1)} %wout_hbm.1, ...), custom_call_target="tpu_custom_call" | custom-call | tf_op jit(solution)/shard_map/pallas_call | solution.py:253
  163.8 1.6 copy.11
  165.4 2.4 %copy.12 = bf16[1,2,768,384]{3,2,1,0:T(8,128)(2,1)} copy(bf16[1,2,768,384]{3,2,1,0:T(8,128)(2,1)} %get-tuple-element.5) | data formatting | bytes 2359296

commit v2 on v1

v2 whole, which is shorter than its diff:
```python
import functools
import math

import jax
import jax.numpy as jnp
from jax import lax
from jax.experimental import pallas as pl
from jax.experimental.pallas import tpu as pltpu
from jax.sharding import PartitionSpec as P

HD = 128
TICKS = 4
SCORE_GAIN = 2.5
EPSILON = 1e-06
PIECE = 16
SHIFT = 16.0
MESH = pl.DeviceIdType.MESH
CUTS = 2
HEAD = ("h0", "h1", "h2", "k3")
TAIL = ("c0", "q", "c1", "c2", "c3", "e0", "e1", "e2", "f0", "e3", "f1", "u", "f2", "f3")


def relay_kernel(
    n_sections, counts_ref, order_ref, x0_ref, kv_hbm, wqkv_hbm, wout_hbm, gain_ref, out_ref, kv_out,
    X, PA, RL, EX, S, W, WO, KV, Q, KF, VF, O, L, wsem, xsem, ss, zs, zs0, rls, exs, ags, osem,
):
    model = X.shape[-1]
    inner = KV.shape[-1]
    heads = inner // HD
    tokens = KV.shape[1]
    NP = PA.shape[1]
    NB = NP // 2
    rows = 4 * PIECE
    width = model // CUTS
    patches = order_ref.shape[0]

    section, sp = lax.axis_index("section"), lax.axis_index("sp")
    zh, y = sp // 4, sp % 4
    later, before = (section + 1) % n_sections, (section + n_sections - 1) % n_sections
    up, down = (section, zh * 4 + (y + 1) % 4), (section, zh * 4 + (y + 3) % 4)
    across = (section, (1 - zh) * 4 + y)
    opposite = (section, zh * 4 + (y + 2) % 4)
    next_same, next_other = (later, zh * 4 + y), (later, (1 - zh) * 4 + y)

    def send(src, dst, send_sem, recv_sem, device):
        pltpu.make_async_remote_copy(
            src_ref=src, dst_ref=dst, send_sem=send_sem, recv_sem=recv_sem, device_id=device, device_id_type=MESH
        ).start()

    def take(view, sem):
        pltpu.make_async_copy(view, view, sem).wait()

    def take_pieces(count, sem):
        take(X.at[pl.ds(0, count // 4)] if count % 4 == 0 else X.at[0, pl.ds(0, count)], sem)

    loads = [pltpu.make_async_copy(kv_hbm.at[0], KV, wsem.at[4])]
    for j in range(3):
        loads.append(pltpu.make_async_copy(wqkv_hbm.at[0, j], W.at[:, pl.ds(j * inner, inner)], wsem.at[j]))
    loads.append(pltpu.make_async_copy(wout_hbm.at[0], WO, wsem.at[3]))
    starts = [
        pltpu.make_async_copy(x0_ref.at[0, pl.ds(k * PIECE, PIECE)], X.at[zh * NB + k, 0], xsem.at[k]) for k in range(NB)
    ]
    for copy in starts + loads:
        copy.start()

    barrier = pltpu.get_barrier_semaphore()
    friends = [up, down, opposite, across, next_same, next_other, (before, zh * 4 + y), (before, (1 - zh) * 4 + y)]
    for device in friends:
        pl.semaphore_signal(barrier, inc=1, device_id=device, device_id_type=MESH)
    pl.semaphore_wait(barrier, len(friends))

    for copy in starts:
        copy.wait()
    for k in range(NB):
        piece = X.at[zh * NB + k, 0]
        send(piece, piece, zs0, exs.at[0, zh * NB + k, 0], across)
    local = lax.broadcasted_iota(jnp.int32, (1, NP * rows), 1)
    slot = (local % rows) // PIECE
    chunk = (y + jnp.where(slot == 1, 1, jnp.where(slot == 2, 3, jnp.where(slot == 3, 2, 0)))) % 4
    within = (local // rows) * PIECE + local % PIECE
    global_row = (within // 32) * 128 + chunk * 32 + within % 32
    token = lax.broadcasted_iota(jnp.int32, (1, tokens), 1)
    gain = gain_ref[...]
    factor = SCORE_GAIN / math.sqrt(HD) * math.log2(math.e)
    shift = SHIFT * math.log2(math.e)

    def gather(t, at, i, c):
        spot = pl.ds(c * width, width)
        for k, device in ((2, up), (1, down), (3, opposite)):
            send(X.at[at, 0, :, spot], X.at[at, k, :, spot], ss.at[t], ags.at[t, i, k], device)

    for i in range(NP):
        ii = (i + zh * NB) % NP
        if i >= NB:
            take(X.at[ii, 0], exs.at[0, ii, 0])
        for c in range(CUTS):
            gather(0, ii, ii, c)
    for copy in loads:
        copy.wait()

    def head_norm(part):
        spread = jnp.mean(part * part, axis=-1, keepdims=True)
        return (part * lax.rsqrt(spread + EPSILON)).astype(jnp.bfloat16)

    def scores(query, keys, bias):
        s = lax.dot_general(query, keys, (((1,), (1,)), ((), ())), preferred_element_type=jnp.float32)
        return jnp.exp2(s * factor + bias)

    def tick(t, _):
        patch = order_ref[(section + TICKS * n_sections - t) % patches]
        length, first = jnp.int32(0), jnp.int32(0)
        for r in range(patches):
            length = length + jnp.where(patch == r, counts_ref[r], 0)
            first = first + jnp.where(r < patch, counts_ref[r], 0)
        held_bias = jnp.where((token >= first) & (token < first + length), -1e30, -shift)
        fresh_bias = jnp.where(global_row < length, -shift, -1e30)

        def stage_f(i):
            @pl.when(t < TICKS - 1)
            def _():
                at = (t + 1) * NP + i
                for c in range(CUTS):
                    part = slice(c * width, (c + 1) * width)
                    take(EX.at[t + 1, i, :, :, pl.ds(c * width, width)], exs.at[t + 1, i, c])
                    total = EX[t + 1, i, 0, :, part].astype(jnp.float32) + EX[t + 1, i, 1, :, part].astype(jnp.float32)
                    X[at, 0, :, part] = total.astype(jnp.bfloat16)
                    gather(t + 1, at, i, c)

        def stage_h(i, whole=True):
            at = t * NP + i
            for k in (1, 2, 3):
                take(X.at[at, k], ags.at[t, i, k])
            x = X[at].reshape(rows, model).astype(jnp.float32)
            spread = jnp.mean(x * x, axis=-1, keepdims=True)
            normed = (x * lax.rsqrt(spread + EPSILON) * gain).astype(jnp.bfloat16)
            here = slice(i * rows, (i + 1) * rows)

            def project(j):
                return jnp.dot(normed, W[:, j * inner : (j + 1) * inner], preferred_element_type=jnp.float32)

            VF[here, :] = project(2).astype(jnp.bfloat16)
            keys = project(1)
            for h in range(heads):
                cols = slice(h * HD, (h + 1) * HD)
                KF[here, cols] = head_norm(keys[:, cols])

            def finish():
                queries = project(0)
                for h in range(heads):
                    cols = slice(h * HD, (h + 1) * HD)
                    query = head_norm(queries[:, cols])
                    Q[here, cols] = query
                    e = scores(query, KV[0, :, cols], held_bias)
                    L[here, cols] = jnp.broadcast_to(jnp.sum(e, axis=-1, keepdims=True), (rows, HD))
                    O[here, cols] = jnp.dot(e.astype(jnp.bfloat16), KV[1, :, cols], preferred_element_type=jnp.float32)

            if whole:
                finish()
            return finish

        def stage_c(i):
            here = slice(i * rows, (i + 1) * rows)
            attended = []
            for h in range(heads):
                cols = slice(h * HD, (h + 1) * HD)
                e = scores(Q[here, cols], KF[:, cols], fresh_bias)
                total = L[here, cols] + jnp.sum(e, axis=-1, keepdims=True)
                mixed = O[here, cols] + jnp.dot(
                    e.astype(jnp.bfloat16), VF[:, cols], preferred_element_type=jnp.float32
                )
                attended.append((mixed / total).astype(jnp.bfloat16))
            attended = jnp.concatenate(attended, axis=1)
            for c in range(CUTS):
                part = slice(c * width, (c + 1) * width)
                spot = pl.ds(c * width, width)
                partial = jnp.dot(attended, WO[:, part], preferred_element_type=jnp.float32)
                PA[t, i, :, :, part] = partial.astype(jnp.bfloat16).reshape(4, PIECE, width)
                for k, device in ((3, opposite), (1, up), (2, down)):
                    send(PA.at[t, i, k, :, spot], RL.at[t, i, k - 1, :, spot], ss.at[t], rls.at[t, i, c], device)

        def stage_e(i):
            for c in range(CUTS):
                part = slice(c * width, (c + 1) * width)
                spot = pl.ds(c * width, width)
                take(RL.at[t, i, :, :, spot], rls.at[t, i, c])
                total = PA[t, i, 0, :, part].astype(jnp.float32)
                for k in range(3):
                    total = total + RL[t, i, k, :, part].astype(jnp.float32)
                total = total + jnp.where(zh == i // NB, X[t * NP + i, 0, :, part].astype(jnp.float32), 0.0)
                S[t, i, :, part] = total.astype(jnp.bfloat16)
                mine = S.at[t, i, :, spot]

                @pl.when(t < TICKS - 1)
                def _():
                    send(mine, EX.at[t + 1, i, 1, :, spot], zs.at[t], exs.at[t + 1, i, c], next_other)
                    send(mine, EX.at[t + 1, i, 0, :, spot], zs.at[t], exs.at[t + 1, i, c], next_same)

                @pl.when(t == TICKS - 1)
                def _():
                    k = i % NB
                    target = (later, (i // NB) * 4 + y)
                    send(mine, EX.at[TICKS, k, zh, :, spot], zs.at[t], exs.at[TICKS, k, c], target)

        def update():
            for b in range(3):
                span = tokens // 3
                at = pl.ds(b * span, span)
                row = lax.broadcasted_iota(jnp.int32, (span, 1), 0) + (b * span - first)
                hit = (row == global_row) & (global_row < length)
                pick = jnp.where(hit, 1.0, 0.0).astype(jnp.bfloat16)
                inside = (row >= 0) & (row < length)
                for part, fresh in ((0, KF), (1, VF)):
                    moved = jnp.dot(pick, fresh[...], preferred_element_type=jnp.float32)
                    kept = KV[part, at, :].astype(jnp.float32)
                    KV[part, at, :] = jnp.where(inside, moved, kept).astype(jnp.bfloat16)

        stages = dict(h=stage_h, c=stage_c, e=stage_e, f=stage_f)
        finish = None
        for step in HEAD + TAIL:
            kind, i = step[0], int(step[1:] or 0)
            if kind == "k":
                finish = stage_h(i, False)
            elif kind == "q":
                finish()
            elif kind == "u":
                update()
            else:
                stages[kind](i)
        return 0

    lax.fori_loop(0, TICKS, tick, 0)
    cache_out = pltpu.make_async_copy(KV, kv_out.at[0], osem)
    cache_out.start()
    for k in range(NB):
        for c in range(CUTS):
            part = slice(c * width, (c + 1) * width)
            take(EX.at[TICKS, k, :, :, pl.ds(c * width, width)], exs.at[TICKS, k, c])
            total = EX[TICKS, k, 0, :, part].astype(jnp.float32) + EX[TICKS, k, 1, :, part].astype(jnp.float32)
            out_ref[0, pl.ds(k * PIECE, PIECE), part] = total.astype(jnp.bfloat16)
    take_pieces(NB, zs0)
    for t in range(TICKS):
        take_pieces(6 * NP, ss.at[t])
        take_pieces(2 * NP if t < TICKS - 1 else NP, zs.at[t])
    cache_out.wait()


def local(n_sections, x0, kv, wqkv, wout, gain, counts, order):
    entries, model = x0.shape[1:]
    tokens, inner = kv.shape[2:]
    NP = 2 * entries // PIECE
    NB = NP // 2
    rows = 8 * entries
    bf16, f32 = jnp.bfloat16, jnp.float32
    piece = (PIECE, model)
    dma = pltpu.SemaphoreType.DMA
    any_space = pl.BlockSpec(memory_space=pl.ANY)
    vmem = pl.BlockSpec(memory_space=pltpu.VMEM)
    smem = pl.BlockSpec(memory_space=pltpu.SMEM)
    return pl.pallas_call(
        functools.partial(relay_kernel, n_sections),
        out_shape=(
            jax.ShapeDtypeStruct((1, entries, model), bf16),
            jax.ShapeDtypeStruct((1, 2, tokens, inner), bf16),
        ),
        in_specs=[smem, smem, any_space, any_space, any_space, any_space, vmem],
        out_specs=(vmem, any_space),
        scratch_shapes=[
            pltpu.VMEM((TICKS * NP, 4) + piece, bf16),
            pltpu.VMEM((TICKS, NP, 4) + piece, bf16),
            pltpu.VMEM((TICKS, NP, 3) + piece, bf16),
            pltpu.VMEM((TICKS + 1, NP, 2) + piece, bf16),
            pltpu.VMEM((TICKS, NP) + piece, bf16),
            pltpu.VMEM((model, 3 * inner), bf16),
            pltpu.VMEM((inner, model), bf16),
            pltpu.VMEM((2, tokens, inner), bf16),
            pltpu.VMEM((rows, inner), bf16),
            pltpu.VMEM((rows, inner), bf16),
            pltpu.VMEM((rows, inner), bf16),
            pltpu.VMEM((rows, inner), f32),
            pltpu.VMEM((rows, inner), f32),
            dma((5,)), dma((NB,)), dma((TICKS,)), dma((TICKS,)), dma,
            dma((TICKS, NP, CUTS)), dma((TICKS + 1, NP, CUTS)), dma((TICKS, NP, 4)), dma,
        ],
        compiler_params=pltpu.CompilerParams(
            collective_id=0, has_side_effects=True, vmem_limit_bytes=56 * 1024 * 1024
        ),
    )(counts, order, x0, kv, jnp.transpose(wqkv, (0, 2, 1, 3)), wout, gain)


def solution(mesh):
    placed = (
        P("section", "sp", None),
        P("section", None, None, "sp"),
        P("section", None, None, "sp"),
        P("section", "sp", None),
        P("section", None),
        P(),
        P(),
    )
    return jax.shard_map(
        functools.partial(local, mesh.shape["section"]),
        mesh=mesh,
        in_specs=placed,
        out_specs=(P("section", "sp", None), P("section", None, None, "sp")),
        check_vma=False,
    )
```

time: 171 us -> 153 us (0.89); the launches traced: 168 us -> 153 us
  Pallas kernels: 163 us -> 149 us
    pallas_call x1, Pallas kernels: 163 us -> 149 us  [local(): pl.pallas_call(functools.partial(relay_kernel, n_sections), out_shape=(ja...]
where the time goes in v2:
time: 153 us
  Pallas kernels  149 us (97%)
  local copies, waits for them, and re-layouts  3.99 us (3%)
    pallas_call x1, Pallas kernels, local(): pl.pallas_call(functools.partial(relay_kernel, n_sections), out_shape=(ja...  149 us
    unnamed x2, local copies, waits for them, and re-layouts  3.99 us

profile of v2, /device:TPU:227, one launch (start us, length us, event | category | flops | bytes accessed | tf_op | source)
XLA Modules:
  0.0 153.2 jit_solution(16742662906963080050)
XLA Ops:
  0.6 148.6 %shard_map.86 = (bf16[1,32,2560]{2,1,0:T(8,128)(2,1)}, bf16[1,2,768,384]{3,2,1,0:T(8,128)(2,1)}) custom-call(s32[4]{0:T(128)} %counts_ref.1, s32[4]{0:T(128)} %order_ref.1, bf16[1,32,2560]{2,1,0:T(8,128)(2,1)} %x0_ref.1, bf16[1,2,768,384]{3,2,1,0:T(8,128)(2,1)} %kv_hbm.1, bf16[1,3,2560,384]{3,2,1,0:T(8,128)(2,1)} %bitcast.1, bf16[1,384,2560]{2,1,0:T(8,128)(2,1)} %wout_hbm.1, ...), custom_call_target="tpu_custom_call" | custom-call | tf_op jit(solution)/shard_map/pallas_call | solution.py:259
  149.2 1.6 %copy.11 = bf16[1,32,2560]{2,1,0:T(8,128)(2,1)} copy(bf16[1,32,2560]{2,1,0:T(8,128)(2,1)} %get-tuple-element.4) | data formatting | bytes 327680
  150.8 2.4 %copy.12 = bf16[1,2,768,384]{3,2,1,0:T(8,128)(2,1)} copy(bf16[1,2,768,384]{3,2,1,0:T(8,128)(2,1)} %get-tuple-element.5) | data formatting | bytes 2359296

commit v3 on v2

--- a/solution.py
+++ b/solution.py
@@ -72,8 +72,9 @@
     for copy in starts:
         copy.wait()
     for k in range(NB):
-        piece = X.at[zh * NB + k, 0]
-        send(piece, piece, zs0, exs.at[0, zh * NB + k, 0], across)
+        for c in range(CUTS):
+            piece = X.at[zh * NB + k, 0, :, pl.ds(c * width, width)]
+            send(piece, piece, zs0, exs.at[0, zh * NB + k, c], across)
     local = lax.broadcasted_iota(jnp.int32, (1, NP * rows), 1)
     slot = (local % rows) // PIECE
     chunk = (y + jnp.where(slot == 1, 1, jnp.where(slot == 2, 3, jnp.where(slot == 3, 2, 0)))) % 4
@@ -86,14 +87,14 @@
 
     def gather(t, at, i, c):
         spot = pl.ds(c * width, width)
-        for k, device in ((2, up), (1, down), (3, opposite)):
+        for k, device in ((3, opposite), (2, up), (1, down)):
             send(X.at[at, 0, :, spot], X.at[at, k, :, spot], ss.at[t], ags.at[t, i, k], device)
 
     for i in range(NP):
         ii = (i + zh * NB) % NP
-        if i >= NB:
-            take(X.at[ii, 0], exs.at[0, ii, 0])
         for c in range(CUTS):
+            if i >= NB:
+                take(X.at[ii, 0, :, pl.ds(c * width, width)], exs.at[0, ii, c])
             gather(0, ii, ii, c)
     for copy in loads:
         copy.wait()
@@ -127,25 +128,24 @@
                     gather(t + 1, at, i, c)
 
         def stage_h(i, whole=True):
-            at = t * NP + i
+            ii = (i + jnp.where(t == 0, zh * NB, 0)) % NP
+            at = t * NP + ii
             for k in (1, 2, 3):
-                take(X.at[at, k], ags.at[t, i, k])
+                take(X.at[at, k], ags.at[t, ii, k])
             x = X[at].reshape(rows, model).astype(jnp.float32)
             spread = jnp.mean(x * x, axis=-1, keepdims=True)
             normed = (x * lax.rsqrt(spread + EPSILON) * gain).astype(jnp.bfloat16)
-            here = slice(i * rows, (i + 1) * rows)
-
-            def project(j):
-                return jnp.dot(normed, W[:, j * inner : (j + 1) * inner], preferred_element_type=jnp.float32)
-
-            VF[here, :] = project(2).astype(jnp.bfloat16)
-            keys = project(1)
+            here = pl.ds(pl.multiple_of(ii * rows, rows), rows)
+
+            pairs = jnp.dot(normed, W[:, inner:], preferred_element_type=jnp.float32)
+            keys = pairs[:, :inner]
+            VF[here, :] = pairs[:, inner:].astype(jnp.bfloat16)
             for h in range(heads):
                 cols = slice(h * HD, (h + 1) * HD)
                 KF[here, cols] = head_norm(keys[:, cols])
 
             def finish():
-                queries = project(0)
+                queries = jnp.dot(normed, W[:, :inner], preferred_element_type=jnp.float32)
                 for h in range(heads):
                     cols = slice(h * HD, (h + 1) * HD)
                     query = head_norm(queries[:, cols])

time: 153 us -> 150 us (0.980)
  Pallas kernels: 149 us -> 144 us
    pallas_call x1, Pallas kernels: 149 us -> 144 us  [local(): pl.pallas_call(functools.partial(relay_kernel, n_sections), out_shape=(ja...]
where the time goes in v3:
time: 150 us; the launch traced here: 149 us
  Pallas kernels  144 us (96%)
  local copies, waits for them, and re-layouts  3.99 us (3%)
    pallas_call x1, Pallas kernels, local(): pl.pallas_call(functools.partial(relay_kernel, n_sections), out_shape=(ja...  144 us
    unnamed x2, local copies, waits for them, and re-layouts  3.99 us

profile of v3, /device:TPU:227, one launch (start us, length us, event | category | flops | bytes accessed | tf_op | source)
XLA Modules:
  0.0 148.9 jit_solution(11790489893893032030)
XLA Ops:
  0.6 144.3 %shard_map.86 = (bf16[1,32,2560]{2,1,0:T(8,128)(2,1)}, bf16[1,2,768,384]{3,2,1,0:T(8,128)(2,1)}) custom-call(s32[4]{0:T(128)} %counts_ref.1, s32[4]{0:T(128)} %order_ref.1, bf16[1,32,2560]{2,1,0:T(8,128)(2,1)} %x0_ref.1, bf16[1,2,768,384]{3,2,1,0:T(8,128)(2,1)} %kv_hbm.1, bf16[1,3,2560,384]{3,2,1,0:T(8,128)(2,1)} %bitcast.1, bf16[1,384,2560]{2,1,0:T(8,128)(2,1)} %wout_hbm.1, ...), custom_call_target="tpu_custom_call" | custom-call | tf_op jit(solution)/shard_map/pallas_call | solution.py:259
  144.9 1.6 %copy.11 = bf16[1,32,2560]{2,1,0:T(8,128)(2,1)} copy(bf16[1,32,2560]{2,1,0:T(8,128)(2,1)} %get-tuple-element.4) | data formatting | bytes 327680
  146.5 2.4 %copy.12 = bf16[1,2,768,384]{3,2,1,0:T(8,128)(2,1)} copy(bf16[1,2,768,384]{3,2,1,0:T(8,128)(2,1)} %get-tuple-element.5) | data formatting | bytes 2359296

commit v4 on v3

--- a/solution.py
+++ b/solution.py
@@ -16,8 +16,8 @@
 SHIFT = 16.0
 MESH = pl.DeviceIdType.MESH
 CUTS = 2
-HEAD = ("h0", "h1", "h2", "k3")
-TAIL = ("c0", "q", "c1", "c2", "c3", "e0", "e1", "e2", "f0", "e3", "f1", "u", "f2", "f3")
+HEAD = ("a0", "h1", "h2", "k3")
+TAIL = ("c0", "q", "c1", "c2", "c3", "e0", "e1", "e2", "f0", "e3", "f1", "u", "f2", "b0", "f3")
 
 
 def relay_kernel(
@@ -107,13 +107,17 @@
         s = lax.dot_general(query, keys, (((1,), (1,)), ((), ())), preferred_element_type=jnp.float32)
         return jnp.exp2(s * factor + bias)
 
-    def tick(t, _):
+    def plan(t):
         patch = order_ref[(section + TICKS * n_sections - t) % patches]
         length, first = jnp.int32(0), jnp.int32(0)
         for r in range(patches):
             length = length + jnp.where(patch == r, counts_ref[r], 0)
             first = first + jnp.where(r < patch, counts_ref[r], 0)
         held_bias = jnp.where((token >= first) & (token < first + length), -1e30, -shift)
+        return length, first, held_bias
+
+    def tick(t, _):
+        length, first, held_now = plan(t)
         fresh_bias = jnp.where(global_row < length, -shift, -1e30)
 
         def stage_f(i):
@@ -127,7 +131,7 @@
                     X[at, 0, :, part] = total.astype(jnp.bfloat16)
                     gather(t + 1, at, i, c)
 
-        def stage_h(i, whole=True):
+        def stage_h(i, whole=True, t=t, held_bias=held_now):
             ii = (i + jnp.where(t == 0, zh * NB, 0)) % NP
             at = t * NP + ii
             for k in (1, 2, 3):
@@ -214,7 +218,17 @@
                     kept = KV[part, at, :].astype(jnp.float32)
                     KV[part, at, :] = jnp.where(inside, moved, kept).astype(jnp.bfloat16)
 
-        stages = dict(h=stage_h, c=stage_c, e=stage_e, f=stage_f)
+        def stage_a(i):
+            @pl.when(t == 0)
+            def _():
+                stage_h(i)
+
+        def stage_b(i):
+            @pl.when(t < TICKS - 1)
+            def _():
+                stage_h(i, True, t + 1, plan(t + 1)[2])
+
+        stages = dict(a=stage_a, b=stage_b, h=stage_h, c=stage_c, e=stage_e, f=stage_f)
         finish = None
         for step in HEAD + TAIL:
             kind, i = step[0], int(step[1:] or 0)

time: 150 us -> 149 us (level)
  no operation moved by 1% of the time
where the time goes in v4:
time: 149 us; the launch traced here: 148 us
  Pallas kernels  143 us (96%)
  local copies, waits for them, and re-layouts  3.99 us (3%)
    pallas_call x1, Pallas kernels, local(): pl.pallas_call(functools.partial(relay_kernel, n_sections), out_shape=(ja...  143 us
    unnamed x2, local copies, waits for them, and re-layouts  3.99 us

profile of v4, /device:TPU:227, one launch (start us, length us, event | category | flops | bytes accessed | tf_op | source)
XLA Modules:
  0.0 147.5 jit_solution(13015159211516852733)
XLA Ops:
  0.6 142.9 %shard_map.86 = (bf16[1,32,2560]{2,1,0:T(8,128)(2,1)}, bf16[1,2,768,384]{3,2,1,0:T(8,128)(2,1)}) custom-call(s32[4]{0:T(128)} %counts_ref.1, s32[4]{0:T(128)} %order_ref.1, bf16[1,32,2560]{2,1,0:T(8,128)(2,1)} %x0_ref.1, bf16[1,2,768,384]{3,2,1,0:T(8,128)(2,1)} %kv_hbm.1, bf16[1,3,2560,384]{3,2,1,0:T(8,128)(2,1)} %bitcast.1, bf16[1,384,2560]{2,1,0:T(8,128)(2,1)} %wout_hbm.1, ...), custom_call_target="tpu_custom_call" | custom-call | tf_op jit(solution)/shard_map/pallas_call | solution.py:273
  143.5 1.6 %copy.11 = bf16[1,32,2560]{2,1,0:T(8,128)(2,1)} copy(bf16[1,32,2560]{2,1,0:T(8,128)(2,1)} %get-tuple-element.4) | data formatting | bytes 327680
  145.1 2.4 %copy.12 = bf16[1,2,768,384]{3,2,1,0:T(8,128)(2,1)} copy(bf16[1,2,768,384]{3,2,1,0:T(8,128)(2,1)} %get-tuple-element.5) | data formatting | bytes 2359296
